TPU v7x, 256 devices: a whole 4x4x8 slice. The times are simulated.
256 devices in a mesh: blk: 32 (over z_lo, y, core), uly: 8 (over z_hi, x).
Axes of the slice: x: 4, y: 4, z: 8 (z_hi: 2, z_lo: 4; z = z_hi * 4 + z_lo), core: 2. Of those that a mesh axis runs over, the one named last changes fastest.
Arguments:
- tokens: bfloat16 [24576, 3072], P(('blk', 'uly')), may hold values from -32 to 32
- qkv_weight: bfloat16 [3072, 3, 3072], P(None, None, 'uly'), may hold values from -1 to 1
- out_weight: bfloat16 [3072, 3072], P('uly'), may hold values from -0.109375 to 0.109375
Outputs:
- mixed: bfloat16 [24576, 3072], P(('blk', 'uly'))
All inputs are finite; a program needn't handle non-finite values.
Results may differ from a plain program's by a relative error of at most 0.011.
Values may be sent and summed in bfloat16 or wider, within the bound.
No kernel may reach another device: no remote copies, remote signals or barrier semaphores. Data moves between devices by JAX's collectives and lax.ppermute only.
A program may use at most 128 MiB of HBM per device.

v0:
```python
import math

import jax
import jax.numpy as jnp
from jax import lax
from jax.sharding import PartitionSpec as P

HEAD_DIM = 128
WINDOW = 4


def from_behind(block, axis, distance):
    devices = range(lax.axis_size(axis))
    route = [((i - distance) % len(devices), i) for i in devices]
    return lax.ppermute(block, axis, route)


def on_device(tokens, qkv_weight, out_weight):
    model_width = tokens.shape[1]
    head_width = qkv_weight.shape[2]
    head_count = head_width // HEAD_DIM
    flat_weight = qkv_weight.reshape(model_width, 3 * head_width)
    projected = jnp.dot(
        lax.all_gather(tokens, "uly", axis=0, tiled=True),
        flat_weight,
        preferred_element_type=jnp.float32,
    ).astype(jnp.bfloat16)
    group_rows = projected.shape[0]
    queries = projected[:, :head_width].reshape(group_rows, head_count, HEAD_DIM)
    own_pairs = projected[:, head_width:]
    scale = 1.0 / math.sqrt(HEAD_DIM)

    def attend(pairs):
        key_block = pairs[:, :head_width].reshape(group_rows, head_count, HEAD_DIM)
        value_block = pairs[:, head_width:].reshape(group_rows, head_count, HEAD_DIM)
        scores = (
            jnp.einsum("qhd,khd->hqk", queries, key_block, preferred_element_type=jnp.float32)
            * scale
        )
        maximum = jnp.max(scores, axis=2)
        weights = jnp.exp(scores - maximum[:, :, None])
        total = jnp.sum(weights, axis=2)
        partial_out = jnp.einsum(
            "hqk,khd->hqd",
            weights.astype(jnp.bfloat16),
            value_block,
            preferred_element_type=jnp.float32,
        )
        return (maximum, total, partial_out)

    def combine(first, second):
        top = jnp.maximum(first[0], second[0])
        first_factor = jnp.exp(first[0] - top)
        second_factor = jnp.exp(second[0] - top)
        total = first[1] * first_factor + second[1] * second_factor
        merged = first[2] * first_factor[:, :, None] + second[2] * second_factor[:, :, None]
        return (top, total, merged)

    state = attend(own_pairs)
    nearer = from_behind(own_pairs, "blk", -1)
    state = combine(state, attend(nearer))
    current = nearer
    for offset in range(2, WINDOW):
        current = from_behind(current, "blk", -1)
        state = combine(state, attend(current))
    attended = (
        (state[2] / state[1][:, :, None])
        .transpose(1, 0, 2)
        .reshape(group_rows, head_width)
        .astype(jnp.bfloat16)
    )
    token_heads = lax.all_to_all(attended, "uly", split_axis=0, concat_axis=1, tiled=True)
    summed = jnp.dot(
        token_heads,
        lax.all_gather(out_weight, "uly", axis=0, tiled=True),
        preferred_element_type=jnp.float32,
    )
    return summed.astype(jnp.bfloat16)


def solution(mesh):
    in_specs = (P(("blk", "uly"), None), P(None, None, "uly"), P("uly", None))
    out_specs = P(("blk", "uly"), None)
    return jax.shard_map(
        on_device, mesh=mesh, in_specs=in_specs, out_specs=out_specs, check_vma=False
    )
```

profile of v0, /device:TPU:1, one launch (start us, length us, event | category | flops | bytes accessed | tf_op | source)
XLA Modules:
  0.0 514.0 jit_solution(7481494473414133684)
XLA Ops:
  6.5 0.0 all-gather.3.cloned.1.call-start
  6.5 0.7 all-gather.3.cloned.1.call-update
  7.3 0.0 all-gather.5.cloned.1.call-start
  7.3 0.7 all-gather.5.cloned.1.call-update
  8.0 10.4 %copy.48 = bf16[3072,3,384]{0,2,1:T(8,128)(2,1)} copy(bf16[3072,3,384]{2,0,1:T(8,128)(2,1)} %param.4) | data formatting | bytes 14155776 | tf_op args[1]
  18.4 109.9 %all-gather.3.cloned.1.call-done = bf16[768,3072]{1,0:T(8,128)(2,1)} async-done(((bf16[96,3072]{1,0:T(8,128)(2,1)}), bf16[768,3072]{1,0:T(8,128)(2,1)}) %all-gather.3.cloned.1.call-update) | async-done | bytes 4718608 | tf_op jit(solution)/shard_map/all_gather | solution.py:24
  128.3 10.2 %convolution_convert_fusion.1 = bf16[768,1152]{1,0:T(8,128)(2,1)S(1)} fusion(bf16[768,3072]{1,0:T(8,128)(2,1)} %all-gather.3.cloned.1.call-done, bf16[3072,1152]{0,1:T(8,128)(2,1)} %bitcast.134), kind=kOutput, calls=%fused_computation.29 | convolution fusion | flops 5436702720 | bytes 13565952 | tf_op jit(solution)/shard_map/dot_general | solution.py:23
  138.6 0.1 slice.45
  138.6 1.2 collective-permute-start
  139.8 15.4 %collective-permute-done = bf16[768,768]{1,0:T(8,128)(2,1)} collective-permute-done((bf16[768,768]{1,0:T(8,128)(2,1)S(1)}, bf16[768,768]{1,0:T(8,128)(2,1)}, u32[]{:S(2)}, u32[]{:S(2)}) %collective-permute-start) | collective-permute-done | bytes 1179680 | tf_op jit(solution)/shard_map/ppermute | solution.py:15
  155.2 20.7 %collective-permute-start.1 = (bf16[768,768]{1,0:T(8,128)(2,1)}, bf16[768,768]{1,0:T(8,128)(2,1)}, u32[]{:S(2)}, u32[]{:S(2)}) collective-permute-start(bf16[768,768]{1,0:T(8,128)(2,1)} %collective-permute-done), channel_id=1, source_target_pairs={{8,0},{16,8},{24,16},{32,24},{40,32},{48,40},{56,48},{64,56},{72,6... | collective-permute-start | bytes 3538952 | tf_op jit(solution)/shard_map/ppermute | solution.py:15
  175.9 0.2 fusion.84
  176.1 0.3 copy.49
  176.4 0.3 copy.50
  176.6 1.1 copy.53
  177.7 4.1 multiply_reduce_fusion.3
  181.8 2.6 fusion.87
  184.3 2.2 copy.56
  186.5 2.1 copy.59
  188.6 2.3 multiply_reduce_fusion.2
  191.0 0.0 copy-start
  191.0 0.0 collective-permute-done.1
  191.0 30.3 %collective-permute-start.2 = (bf16[768,768]{1,0:T(8,128)(2,1)}, bf16[768,768]{1,0:T(8,128)(2,1)}, u32[]{:S(2)}, u32[]{:S(2)}) collective-permute-start(bf16[768,768]{1,0:T(8,128)(2,1)} %collective-permute-done.1), channel_id=1, source_target_pairs={{8,0},{16,8},{24,16},{32,24},{40,32},{48,40},{56,48},{64,56},{72,6... | collective-permute-start | bytes 3538952 | tf_op jit(solution)/shard_map/ppermute | solution.py:15
  221.3 0.0 slice-done
  221.3 0.0 slice-done.1
  221.4 3.0 fusion
  224.3 0.0 copy-done
  224.3 1.4 fusion.86
  225.7 0.3 copy.62
  225.9 1.1 copy.65
  227.1 4.0 multiply_reduce_fusion.1
  231.0 0.0 collective-permute-done.2
  231.0 1.4 fusion.85
  232.4 1.1 copy.68
  233.5 1.1 copy.71
  234.5 2.4 multiply_reduce_fusion
  236.9 0.0 copy-start.6
  236.9 0.0 slice-start.4
  236.9 0.8 copy-done.1
  237.7 0.0 slice-start.5
  237.7 2.4 fusion.4
  240.1 0.0 copy-start.3
  240.1 0.0 copy-done.6
  240.1 0.0 copy-done.8
  240.1 0.0 copy-done.9
  240.2 0.7 fusion.67
  240.8 0.0 slice-done.2
  240.8 2.3 slice-done.3
  243.1 0.0 copy-done.2
  243.1 2.9 fusion.60
  246.0 0.0 slice-done.4
  246.0 0.0 slice-done.5
  246.0 0.0 copy-done.3
  246.0 3.6 fusion.57
  249.6 0.0 copy-start.5
  249.6 0.0 copy-start.7
  249.6 2.3 fusion.48
  252.0 2.3 divide_convert_fusion
  254.2 0.5 copy.93
  254.8 0.5 reshape.126
  255.3 29.7 %all_to_all.16 = bf16[8,96,384]{2,1,0:T(8,128)(2,1)S(1)} all-to-all(bf16[8,96,384]{2,1,0:T(8,128)(2,1)S(1)} %reshape.126), channel_id=1, replica_groups=mesh['blk'=32,'uly'=8] {'uly'}, dimensions={0} | all-to-all | bytes 1179648 | tf_op jit(solution)/shard_map/all_to_all | solution.py:72
  285.0 0.1 copy.95
  285.1 211.9 %all-gather.5.cloned.1.call-done = bf16[3072,3072]{1,0:T(8,128)(2,1)} async-done(((bf16[384,3072]{1,0:T(8,128)(2,1)}), bf16[3072,3072]{1,0:T(8,128)(2,1)}) %all-gather.5.cloned.1.call-update) | async-done | bytes 18874384 | tf_op jit(solution)/shard_map/all_gather | solution.py:75
  496.9 10.3 %convolution_convert_fusion = bf16[96,3072]{1,0:T(8,128)(2,1)} fusion(bf16[96,3072]{1,0:T(8,128)(2,1)S(1)} %bitcast.135, bf16[3072,3072]{1,0:T(8,128)(2,1)} %all-gather.5.cloned.1.call-done), kind=kOutput, calls=%fused_computation.28 | convolution fusion | flops 1812234240 | bytes 20054016 | tf_op jit(solution)/shard_map/dot_general | solution.py:73
  (23 shorter events, 0.0 us)
Async XLA Ops:
  6.5 121.8 %all-gather.3.cloned.1.call-start = ((), (), s32[]{:S(2)}) async-start(), calls=%async_computation.1 | async-start | bytes 5308416 | tf_op jit(solution)/shard_map/all_gather | solution.py:24
  7.3 489.7 %all-gather.5.cloned.1.call-start = ((), (), s32[]{:S(2)}) async-start(), calls=%async_computation.2 | async-start | bytes 21233664 | tf_op jit(solution)/shard_map/all_gather | solution.py:75
  138.6 16.6 %collective-permute-start = (bf16[768,768]{1,0:T(8,128)(2,1)S(1)}, bf16[768,768]{1,0:T(8,128)(2,1)}, u32[]{:S(2)}, u32[]{:S(2)}) collective-permute-start(bf16[768,768]{1,0:T(8,128)(2,1)S(1)} %slice.45), channel_id=1, source_target_pairs={{8,0},{16,8},{24,16},{32,24},{40,32},{48,40},{56,48},{64,56},{72,6... | collective-permute-start | bytes 3538952 | tf_op jit(solution)/shard_map/ppermute | solution.py:15
  155.2 35.8 %collective-permute-start.1 = (bf16[768,768]{1,0:T(8,128)(2,1)}, bf16[768,768]{1,0:T(8,128)(2,1)}, u32[]{:S(2)}, u32[]{:S(2)}) collective-permute-start(bf16[768,768]{1,0:T(8,128)(2,1)} %collective-permute-done), channel_id=1, source_target_pairs={{8,0},{16,8},{24,16},{32,24},{40,32},{48,40},{56,48},{64,56},{72,6... | collective-permute-start | bytes 3538952 | tf_op jit(solution)/shard_map/ppermute | solution.py:15
  181.8 39.6 %slice-start = ((s8[7077888]{0:T(1024)(128)(4,1)}), s8[2883584]{0:T(1024)(128)(4,1)S(1)}, s32[]{:S(2)}) async-start(s8[7077888]{0:T(1024)(128)(4,1)} %bitcast.124), calls=%async_computation.3 | async-start | bytes 5767168
  188.6 32.7 %slice-start.1 = ((s8[7077888]{0:T(1024)(128)(4,1)}), s8[4194304]{0:T(1024)(128)(4,1)S(1)}, s32[]{:S(2)}) async-start(s8[7077888]{0:T(1024)(128)(4,1)} %bitcast.124), calls=%async_computation.4 | async-start | bytes 8388608
  191.0 33.3 %copy-start = (f32[3,768,768]{1,2,0:T(8,128)}, f32[3,768,768]{1,2,0:T(8,128)S(1)}, u32[]{:S(2)}) copy-start(f32[3,768,768]{1,2,0:T(8,128)S(1)} %get-tuple-element.28) | copy-start | bytes 21233668
  191.0 40.0 %collective-permute-start.2 = (bf16[768,768]{1,0:T(8,128)(2,1)}, bf16[768,768]{1,0:T(8,128)(2,1)}, u32[]{:S(2)}, u32[]{:S(2)}) collective-permute-start(bf16[768,768]{1,0:T(8,128)(2,1)} %collective-permute-done.1), channel_id=1, source_target_pairs={{8,0},{16,8},{24,16},{32,24},{40,32},{48,40},{56,48},{64,56},{72,6... | collective-permute-start | bytes 3538952 | tf_op jit(solution)/shard_map/ppermute | solution.py:15
  234.5 3.2 copy-start.1
  234.5 6.3 %slice-start.2 = ((s8[7077888]{0:T(1024)(128)(4,1)}), s8[4194304]{0:T(1024)(128)(4,1)S(1)}, s32[]{:S(2)}) async-start(s8[7077888]{0:T(1024)(128)(4,1)} %bitcast.126), calls=%async_computation.5 | async-start | bytes 8388608
  236.9 3.2 copy-start.6
  236.9 9.0 %slice-start.4 = ((s8[7077888]{0:T(1024)(128)(4,1)}), s8[4194304]{0:T(1024)(128)(4,1)S(1)}, s32[]{:S(2)}) async-start(s8[7077888]{0:T(1024)(128)(4,1)} %bitcast.128), calls=%async_computation.7 | async-start | bytes 8388608
  237.7 2.4 copy-start.8
  237.7 2.4 copy-start.9
  237.7 5.4 %slice-start.3 = ((s8[7077888]{0:T(1024)(128)(4,1)}), s8[2883584]{0:T(1024)(128)(4,1)S(1)}, s32[]{:S(2)}) async-start(s8[7077888]{0:T(1024)(128)(4,1)} %bitcast.126), calls=%async_computation.6 | async-start | bytes 5767168
  237.7 5.4 %copy-start.2 = (bf16[768,384]{0,1:T(8,128)(2,1)S(1)}, bf16[768,384]{0,1:T(8,128)(2,1)}, u32[]{:S(2)}) copy-start(bf16[768,384]{0,1:T(8,128)(2,1)} %copy.53) | copy-start | bytes 1769476
  237.7 8.2 %slice-start.5 = ((s8[7077888]{0:T(1024)(128)(4,1)}), s8[2883584]{0:T(1024)(128)(4,1)S(1)}, s32[]{:S(2)}) async-start(s8[7077888]{0:T(1024)(128)(4,1)} %bitcast.128), calls=%async_computation.8 | async-start | bytes 5767168
  240.1 5.9 %copy-start.3 = (bf16[768,384]{0,1:T(8,128)(2,1)S(1)}, bf16[768,384]{0,1:T(8,128)(2,1)}, u32[]{:S(2)}) copy-start(bf16[768,384]{0,1:T(8,128)(2,1)} %copy.59) | copy-start | bytes 1769476
  245.9 3.7 copy-start.4
  245.9 3.7 copy-start.10
  245.9 3.7 copy-start.11
  249.6 2.4 copy-start.5
  249.6 2.4 copy-start.7
  249.6 2.4 copy-start.12
  249.6 2.4 copy-start.13
Sparse Core Ops, SparseCore 0:
  10.0 118.3 all-gather.2
  131.0 365.9 all-gather.4
where the time goes:
time: 515 us; the launch traced here: 514 us
  waiting for transfers between devices  339 us (66%)
  starting transfers between devices  52.3 us (10%)
  matrix products  44.2 us (9%)
  blocking collectives  29.7 us (6%)
  local copies, waits for them, and re-layouts  29.6 us (6%)
  between operations  13.7 us (3%)
  other arithmetic  5.98 us (1%)
    all_gather x1, waiting for transfers between devices, on_device(): lax.all_gather(out_weight, 'uly', axis=0, tiled=True)  212 us
    all_gather x1, waiting for transfers between devices, on_device(): lax.all_gather(tokens, 'uly', axis=0, tiled=True)  110 us
    ppermute x3, starting transfers between devices, from_behind(): return lax.ppermute(block, axis, route)  52.3 us
    all_to_all x1, blocking collectives, on_device(): lax.all_to_all(attended, 'uly', split_axis=0, concat_axis=1, tiled=True)  29.7 us
    ppermute x3, waiting for transfers between devices, from_behind(): return lax.ppermute(block, axis, route)  15.4 us
    unnamed x41, local copies, waits for them, and re-layouts  13.5 us
    dot_general x4, matrix products, attend(): jnp.einsum('qhd,khd->hqk', queries, key_block, preferred_element_type=jnp...  12.7 us
    dot_general x4, matrix products, attend(): jnp.einsum('hqk,khd->hqd', weights.astype(jnp.bfloat16), value_block, pre...  11 us
  transfers between devices with their start and end apart: 5, of which 3 were waited for; matrix products, arithmetic and copies ran while one was open for 13% of the time, Pallas kernels for 0%

commit v1 on v0

v1 whole, which is shorter than its diff:
```python
import functools
import math

import jax
import jax.numpy as jnp
from jax import lax
from jax.experimental import pallas as pl
from jax.experimental.pallas import tpu as pltpu
from jax.sharding import PartitionSpec as P

HEAD_DIM = 128
Z_LO, Y, CORE, Z_HI, X = 4, 4, 2, 2, 4
BOTH = ("blk", "uly")
EXP2_SCALE = math.log2(math.e) / math.sqrt(HEAD_DIM)
VMEM_LIMIT = 48 * 1024 * 1024


def route(move):
    pairs = []
    for place in range(Z_LO * Y * CORE * Z_HI * X):
        blk, uly = divmod(place, Z_HI * X)
        chip, core = divmod(blk, CORE)
        z_hi, x = divmod(uly, X)
        target = move(chip, core, z_hi, x)
        if target is not None:
            chip2, core2, z_hi2, x2 = target
            blk2 = (chip2 % (Z_LO * Y)) * CORE + core2
            pairs.append((place, blk2 * Z_HI * X + (z_hi2 % Z_HI) * X + x2 % X))
    return pairs


def send(block, move):
    return lax.ppermute(block, BOTH, route(move))


def first_way(chip, core, z_hi, x):
    return chip, core, z_hi, x + (1 if core == 0 else -1)


def other_way(chip, core, z_hi, x):
    return chip, core, z_hi, x - (1 if core == 0 else -1)


def across_z(chip, core, z_hi, x):
    return chip, core, z_hi + 1, x


def other_core(chip, core, z_hi, x):
    return chip, 1 - core, z_hi, x


def chip_before(chip, core, z_hi, x):
    return chip - 1, core, z_hi, x


def last_group(chip, core, z_hi, x):
    return (chip, 0, z_hi, x) if core == 1 else (chip - 1, 1, z_hi, x)


def project_kernel(own, first, other, far, weight, queries, pairs, rows):
    part = pl.program_id(0)
    n = own.shape[0]

    @pl.when(part == 0)
    def _():
        for slot, ref in enumerate((own, first, other, far)):
            rows[slot * n : (slot + 1) * n, :] = ref[...]

    result = jnp.dot(rows[...], weight[0], preferred_element_type=jnp.float32).astype(jnp.bfloat16)

    @pl.when(part == 0)
    def _():
        queries[...] = result

    @pl.when(part > 0)
    def _():
        pairs[...] = result


def project(slots, weight):
    n, width = slots[0].shape
    head_width = weight.shape[2]
    m = 4 * n
    return pl.pallas_call(
        project_kernel,
        grid=(3,),
        in_specs=[pl.BlockSpec((n, width), lambda j: (0, 0))] * 4
        + [pl.BlockSpec((1, width, head_width), lambda j: (j, 0, 0))],
        out_specs=[
            pl.BlockSpec((m, head_width), lambda j: (0, 0)),
            pl.BlockSpec((m, head_width), lambda j: (0, jnp.maximum(j - 1, 0))),
        ],
        out_shape=[
            jax.ShapeDtypeStruct((m, head_width), jnp.bfloat16),
            jax.ShapeDtypeStruct((m, 2 * head_width), jnp.bfloat16),
        ],
        scratch_shapes=[pltpu.VMEM((m, width), jnp.bfloat16)],
        compiler_params=pltpu.CompilerParams(vmem_limit_bytes=VMEM_LIMIT),
        cost_estimate=pl.CostEstimate(
            flops=2 * m * width * 3 * head_width, bytes_accessed=2 * 3 * width * head_width, transcendentals=0
        ),
    )(*slots, weight)


def attend_kernel(n_queries, n_pairs, *refs):
    queries = refs[:n_queries]
    pairs = refs[n_queries : n_queries + n_pairs]
    out, q_all, kv_all, sems = refs[n_queries + n_pairs :]
    m, head_width = queries[0].shape
    rows = pairs[0].shape[0]
    copies = [pltpu.make_async_copy(ref, q_all.at[i], sems.at[i]) for i, ref in enumerate(queries)]
    copies += [
        pltpu.make_async_copy(ref, kv_all.at[pl.ds(i * rows, rows), :], sems.at[n_queries + i])
        for i, ref in enumerate(pairs)
    ]
    for copy in copies:
        copy.start()
    for copy in copies:
        copy.wait()
    keys = n_pairs * rows
    step = 768

    @pl.loop(0, n_queries)
    def _(chunk):
        for head in range(head_width // HEAD_DIM):
            columns = slice(head * HEAD_DIM, (head + 1) * HEAD_DIM)
            values = slice(head_width + head * HEAD_DIM, head_width + (head + 1) * HEAD_DIM)
            query = q_all[chunk, :, columns]
            scores = [
                lax.dot_general(
                    query,
                    kv_all[k : k + step, columns],
                    (((1,), (1,)), ((), ())),
                    preferred_element_type=jnp.float32,
                )
                for k in range(0, keys, step)
            ]
            top = functools.reduce(jnp.maximum, [jnp.max(s, axis=1, keepdims=True) for s in scores])
            total = jnp.zeros((m, 1), jnp.float32)
            mixed = jnp.zeros((m, HEAD_DIM), jnp.float32)
            for i, s in enumerate(scores):
                weights = jnp.exp2((s - top) * EXP2_SCALE)
                total = total + jnp.sum(weights, axis=1, keepdims=True)
                mixed = mixed + jnp.dot(
                    weights.astype(jnp.bfloat16),
                    kv_all[i * step : (i + 1) * step, values],
                    preferred_element_type=jnp.float32,
                )
            out[chunk, :, columns] = (mixed / total).astype(jnp.bfloat16)


def attend(queries, pairs):
    m, head_width = queries[0].shape
    rows = pairs[0].shape[0]
    keys = len(pairs) * rows
    pairs_work = len(queries) * m * keys * head_width
    return pl.pallas_call(
        functools.partial(attend_kernel, len(queries), len(pairs)),
        in_specs=[pl.BlockSpec(memory_space=pl.ANY)] * (len(queries) + len(pairs)),
        out_specs=pl.BlockSpec(memory_space=pltpu.VMEM),
        out_shape=jax.ShapeDtypeStruct((len(queries), m, head_width), jnp.bfloat16),
        scratch_shapes=[
            pltpu.VMEM((len(queries), m, head_width), jnp.bfloat16),
            pltpu.VMEM((keys, 2 * head_width), jnp.bfloat16),
            pltpu.SemaphoreType.DMA((len(queries) + len(pairs),)),
        ],
        compiler_params=pltpu.CompilerParams(vmem_limit_bytes=VMEM_LIMIT),
        cost_estimate=pl.CostEstimate(
            flops=4 * pairs_work, bytes_accessed=4 * keys * head_width, transcendentals=pairs_work // HEAD_DIM
        ),
    )(*queries, *pairs)


def on_device(tokens, qkv_weight, out_weight):
    rows = tokens.shape[0]
    half = rows // 2
    own_chunks = [tokens[:half], tokens[half:]]
    far_chunks = [send(chunk, across_z) for chunk in own_chunks]
    weight = jnp.transpose(qkv_weight, (1, 0, 2))

    queries, all_pairs = [], []
    for chunk in own_chunks + far_chunks:
        first = send(chunk, first_way)
        other = send(chunk, other_way)
        far = send(first, first_way)
        chunk_queries, own_pairs = project((chunk, first, other, far), weight)
        queries.append(chunk_queries)
        two_on = send(own_pairs, chip_before)
        swapped = send(two_on, other_core)
        is_second = lax.axis_index("blk") % CORE == 1
        last = send(jnp.where(is_second, own_pairs, two_on), last_group)
        all_pairs += [own_pairs, two_on, swapped, last]

    share = out_weight.shape[0] // (Y * CORE)
    place = lax.axis_index("blk") % (Y * CORE)
    piece = lax.dynamic_slice_in_dim(out_weight, place * share, share, 0)
    piece = send(piece, across_z)
    groups = [[i * Y * CORE + j for j in range(Y * CORE)] for i in range(Z_LO)]
    partner_weight = lax.all_gather(piece, "blk", axis=0, tiled=True, axis_index_groups=groups)

    attended = attend(queries, all_pairs)
    outputs = []
    for part in range(2):
        received = send(attended[2 + part], across_z)
        partial = jnp.dot(attended[part], out_weight, preferred_element_type=jnp.float32) + jnp.dot(
            received, partner_weight, preferred_element_type=jnp.float32
        )
        own, first, other, far = (partial[i * half : (i + 1) * half] for i in range(4))
        from_far = send(far.astype(jnp.bfloat16), other_way)
        from_other = send(other.astype(jnp.bfloat16), first_way)
        from_first = send((first + from_far.astype(jnp.float32)).astype(jnp.bfloat16), other_way)
        outputs.append(
            (own + from_other.astype(jnp.float32) + from_first.astype(jnp.float32)).astype(jnp.bfloat16)
        )
    return jnp.concatenate(outputs, axis=0)


def solution(mesh):
    in_specs = (P(("blk", "uly"), None), P(None, None, "uly"), P("uly", None))
    out_specs = P(("blk", "uly"), None)
    return jax.shard_map(
        on_device, mesh=mesh, in_specs=in_specs, out_specs=out_specs, check_vma=False
    )
```

time: 515 us -> 182 us (0.35)
  waiting for transfers between devices: 339 us -> 42.4 us
  matrix products: 44.2 us -> 4.91 us
  Pallas kernels: 0 us -> 34.9 us
  blocking collectives: 29.7 us -> 0 us
  local copies, waits for them, and re-layouts: 29.6 us -> 4.26 us
  starting transfers between devices: 52.3 us -> 77.4 us
    all_gather x2 -> x1, waiting for transfers between devices: 322 us -> 0.01 us  [on_device(): lax.all_gather(piece, 'blk', axis=0, tiled=True, axis_index_groups=groups)]
    dot_general x10 -> x4, matrix products: 44.2 us -> 4.91 us  [the longest x2 3.25 us: on_device(): jnp.dot(received, partner_weight, preferred_element_type=jnp.float32)]
    pallas_call x0 -> x5, Pallas kernels: none -> 34.9 us  [the longest x4 21.1 us: project(): pl.pallas_call(project_kernel, grid=(3,), in_specs=[pl.BlockSpec((n, widt...]
    all_to_all x1 -> x0, blocking collectives: 29.7 us -> none  [on_device(): lax.all_to_all(attended, 'uly', split_axis=0, concat_axis=1, tiled=True)]
    ppermute x3 -> x35, waiting for transfers between devices: 15.4 us -> 42.4 us  [send(): return lax.ppermute(block, BOTH, route(move))]
    ppermute x3 -> x35, starting transfers between devices: 52.3 us -> 77.4 us  [send(): return lax.ppermute(block, BOTH, route(move))]
    slice x14 -> x3, local copies, waits for them, and re-layouts: 15 us -> 1.17 us  [the longest x1 1.09 us: on_device(): own_chunks = [tokens[:half], tokens[half:]]]
    unnamed x41 -> x10, local copies, waits for them, and re-layouts: 13.5 us -> 3.03 us
  transfers between devices with their start and end apart: 5 -> 36, of which waited for: 3 -> 11; matrix products, arithmetic and copies ran while one was open for 13% -> 4% of each run, Pallas kernels for 0% -> 19%
where the time goes in v1:
time: 182 us; the launch traced here: 180 us
  starting transfers between devices  77.4 us (43%)
  waiting for transfers between devices  42.4 us (23%)
  Pallas kernels  34.9 us (19%)
  between operations  13.6 us (7%)
  matrix products  4.91 us (3%)
  local copies, waits for them, and re-layouts  4.26 us (2%)
  other arithmetic  2.24 us (1%)
    ppermute x35, starting transfers between devices, send(): return lax.ppermute(block, BOTH, route(move))  77.4 us
    ppermute x35, waiting for transfers between devices, send(): return lax.ppermute(block, BOTH, route(move))  42.4 us
    pallas_call x4, Pallas kernels, project(): pl.pallas_call(project_kernel, grid=(3,), in_specs=[pl.BlockSpec((n, widt...  21.1 us
    pallas_call x1, Pallas kernels, attend(): pl.pallas_call(functools.partial(attend_kernel, len(queries), len(pairs))...  13.8 us
  transfers between devices with their start and end apart: 36, of which 11 were waited for; matrix products, arithmetic and copies ran while one was open for 4% of the time, Pallas kernels for 19%

profile of v1, /device:TPU:1, one launch (start us, length us, event | category | flops | bytes accessed | tf_op | source)
XLA Modules:
  0.0 179.7 jit_solution(1148350607723740449)
XLA Ops:
  6.5 1.7 copy-done
  8.2 7.8 %collective-permute-start.27 = (bf16[48,3072]{1,0:T(8,128)(2,1)S(1)}, bf16[48,3072]{1,0:T(8,128)(2,1)S(1)}, u32[]{:S(2)}, u32[]{:S(2)}) collective-permute-start(bf16[48,3072]{1,0:T(8,128)(2,1)S(1)} %constant_dynamic-slice_fusion), channel_id=1, source_target_pairs={{0,4},{1,5},{2,6},{3,7},{4,0},{5,1},{6,2},{7,3},{8,12},{9,13},{10,... | collective-permute-start | bytes 884744 | tf_op jit(solution)/shard_map/ppermute | solution.py:33
  16.1 7.2 %collective-permute-done.27 = bf16[48,3072]{1,0:T(8,128)(2,1)S(1)} collective-permute-done((bf16[48,3072]{1,0:T(8,128)(2,1)S(1)}, bf16[48,3072]{1,0:T(8,128)(2,1)S(1)}, u32[]{:S(2)}, u32[]{:S(2)}) %collective-permute-start.27) | collective-permute-done | bytes 294944 | tf_op jit(solution)/shard_map/ppermute | solution.py:33
  23.2 0.7 copy-done.4
  23.9 0.0 all-gather.2.cloned.1.call-update
  24.0 1.1 fusion.8
  25.1 3.1 %collective-permute-start = (bf16[48,3072]{1,0:T(8,128)(2,1)S(1)}, bf16[48,3072]{1,0:T(8,128)(2,1)S(1)}, u32[]{:S(2)}, u32[]{:S(2)}) collective-permute-start(bf16[48,3072]{1,0:T(8,128)(2,1)S(1)} %get-tuple-element.28.own), channel_id=1, source_target_pairs={{0,1},{1,2},{2,3},{3,0},{4,5},{5,6},{6,7},{7,4},{8,11},{9,8},{10,9... | collective-permute-start | bytes 884744 | tf_op jit(solution)/shard_map/ppermute | solution.py:33
  28.2 0.0 collective-permute-start.1
  28.2 2.7 %collective-permute-start.3 = (bf16[48,3072]{1,0:T(8,128)(2,1)S(1)}, bf16[48,3072]{1,0:T(8,128)(2,1)}, u32[]{:S(2)}, u32[]{:S(2)}) collective-permute-start(bf16[48,3072]{1,0:T(8,128)(2,1)S(1)} %get-tuple-element.27.own), channel_id=1, source_target_pairs={{0,1},{1,2},{2,3},{3,0},{4,5},{5,6},{6,7},{7,4},{8,11},{9,8},{10,9... | collective-permute-start | bytes 884744 | tf_op jit(solution)/shard_map/ppermute | solution.py:33
  30.8 5.1 %collective-permute-start.6 = (bf16[48,3072]{1,0:T(8,128)(2,1)S(1)}, bf16[48,3072]{1,0:T(8,128)(2,1)S(1)}, u32[]{:S(2)}, u32[]{:S(2)}) collective-permute-start(bf16[48,3072]{1,0:T(8,128)(2,1)S(1)} %get-tuple-element.28.own), channel_id=1, source_target_pairs={{0,4},{1,5},{2,6},{3,7},{4,0},{5,1},{6,2},{7,3},{8,12},{9,13},{10,... | collective-permute-start | bytes 884744 | tf_op jit(solution)/shard_map/ppermute | solution.py:33
  35.9 0.3 collective-permute-start.10
  36.2 0.0 collective-permute-done.first
  36.2 0.0 collective-permute-start.2
  36.2 2.2 %collective-permute-done.1.other = bf16[48,3072]{1,0:T(8,128)(2,1)S(1)} collective-permute-done((bf16[48,3072]{1,0:T(8,128)(2,1)S(1)}, bf16[48,3072]{1,0:T(8,128)(2,1)S(1)}, u32[]{:S(2)}, u32[]{:S(2)}) %collective-permute-start.1) | collective-permute-done | bytes 294944 | tf_op jit(solution)/shard_map/ppermute | solution.py:33
  38.5 2.9 %collective-permute-start.5 = (bf16[48,3072]{1,0:T(8,128)(2,1)}, bf16[48,3072]{1,0:T(8,128)(2,1)}, u32[]{:S(2)}, u32[]{:S(2)}) collective-permute-start(bf16[48,3072]{1,0:T(8,128)(2,1)} %collective-permute-done.3.first), channel_id=1, source_target_pairs={{0,1},{1,2},{2,3},{3,0},{4,5},{5,6},{6,7},{7,4},{8,11},{9,8},{10,9... | collective-permute-start | bytes 884744 | tf_op jit(solution)/shard_map/ppermute | solution.py:33
  41.4 0.0 collective-permute-start.7
  41.4 7.3 %collective-permute-done.10.own = bf16[48,3072]{1,0:T(8,128)(2,1)S(1)} collective-permute-done((bf16[48,3072]{1,0:T(8,128)(2,1)S(1)}, bf16[48,3072]{1,0:T(8,128)(2,1)S(1)}, u32[]{:S(2)}, u32[]{:S(2)}) %collective-permute-start.10) | collective-permute-done | bytes 294944 | tf_op jit(solution)/shard_map/ppermute | solution.py:33
  48.7 5.7 %shard_map.37 = (bf16[192,384]{1,0:T(8,128)(2,1)S(1)}, bf16[192,768]{1,0:T(8,128)(2,1)}) custom-call(bf16[48,3072]{1,0:T(8,128)(2,1)S(1)} %get-tuple-element.28.own, bf16[48,3072]{1,0:T(8,128)(2,1)S(1)} %collective-permute-done.first, bf16[48,3072]{1,0:T(8,128)(2,1)S(1)} %collective-permute-done.1.other, bf16[48,3072]{1,0:T(8,128)(2,1)S(1)} %collective-permute-done.2.far, ...), custom_call_target="tpu_custom_call" | custom-call | flops 1358954496 | bytes 7077888 | tf_op jit(solution)/shard_map/pallas_call | solution.py:84
  54.5 0.7 copy-done.1
  55.2 8.2 %collective-permute-start.14 = (bf16[192,768]{1,0:T(8,128)(2,1)}, bf16[192,768]{1,0:T(8,128)(2,1)}, u32[]{:S(2)}, u32[]{:S(2)}) collective-permute-start(bf16[192,768]{1,0:T(8,128)(2,1)} %get-tuple-element.17.refs_4_), channel_id=1, source_target_pairs={{0,240},{1,241},{2,242},{3,243},{4,244},{5,245},{6,246},{7,247},{8... | collective-permute-start | bytes 884744 | tf_op jit(solution)/shard_map/ppermute | solution.py:33
  63.4 0.4 collective-permute-start.8
  63.8 0.5 collective-permute-start.12
  64.3 2.2 %collective-permute-start.9 = (bf16[48,3072]{1,0:T(8,128)(2,1)}, bf16[48,3072]{1,0:T(8,128)(2,1)S(1)}, u32[]{:S(2)}, u32[]{:S(2)}) collective-permute-start(bf16[48,3072]{1,0:T(8,128)(2,1)} %collective-permute-done.7.first), channel_id=1, source_target_pairs={{0,1},{1,2},{2,3},{3,0},{4,5},{5,6},{6,7},{7,4},{8,11},{9,8},{10,9... | collective-permute-start | bytes 884744 | tf_op jit(solution)/shard_map/ppermute | solution.py:33
  66.5 5.2 %shard_map.38 = (bf16[192,384]{1,0:T(8,128)(2,1)S(1)}, bf16[192,768]{1,0:T(8,128)(2,1)S(1)}) custom-call(bf16[48,3072]{1,0:T(8,128)(2,1)S(1)} %get-tuple-element.27.own, bf16[48,3072]{1,0:T(8,128)(2,1)} %collective-permute-done.3.first, bf16[48,3072]{1,0:T(8,128)(2,1)} %collective-permute-done.4.other, bf16[48,3072]{1,0:T(8,128)(2,1)} %collective-permute-done.5.far, ...), custom_call_target="tpu_custom_call" | custom-call | flops 1358954496 | bytes 7077888 | tf_op jit(solution)/shard_map/pallas_call | solution.py:84
  71.7 0.5 collective-permute-start.17
  72.3 1.1 collective-permute-start.13
  73.4 1.0 broadcast_select_fusion.3
  74.4 13.9 %collective-permute-start.16 = (bf16[192,768]{1,0:T(8,128)(2,1)S(1)}, bf16[192,768]{1,0:T(8,128)(2,1)S(1)}, u32[]{:S(2)}, u32[]{:S(2)}) collective-permute-start(bf16[192,768]{1,0:T(8,128)(2,1)S(1)} %broadcast_select_fusion.3), channel_id=1, source_target_pairs={{0,248},{1,249},{2,250},{3,251},{4,252},{5,253},{6,254},{7,255},{8... | collective-permute-start | bytes 884744 | tf_op jit(solution)/shard_map/ppermute | solution.py:33
  88.2 5.1 %shard_map.39 = (bf16[192,384]{1,0:T(8,128)(2,1)S(1)}, bf16[192,768]{1,0:T(8,128)(2,1)S(1)}) custom-call(bf16[48,3072]{1,0:T(8,128)(2,1)S(1)} %collective-permute-done.6.own, bf16[48,3072]{1,0:T(8,128)(2,1)} %collective-permute-done.7.first, bf16[48,3072]{1,0:T(8,128)(2,1)S(1)} %collective-permute-done.8.other, ...), custom_call_target="tpu_custom_call" | custom-call | flops 1358954496 | bytes 7077888 | tf_op jit(solution)/shard_map/pallas_call | solution.py:84
  93.3 0.2 collective-permute-start.20
  93.5 5.0 %shard_map.40 = (bf16[192,384]{1,0:T(8,128)(2,1)S(1)}, bf16[192,768]{1,0:T(8,128)(2,1)S(1)}) custom-call(bf16[48,3072]{1,0:T(8,128)(2,1)S(1)} %collective-permute-done.10.own, bf16[48,3072]{1,0:T(8,128)(2,1)S(1)} %collective-permute-done.11.first, bf16[48,3072]{1,0:T(8,128)(2,1)S(1)} %collective-permute-done.12.other, ...), custom_call_target="tpu_custom_call" | custom-call | flops 1358954496 | bytes 7077888 | tf_op jit(solution)/shard_map/pallas_call | solution.py:84
  98.6 0.3 collective-permute-start.23
  98.9 2.4 %collective-permute-start.19 = (bf16[192,768]{1,0:T(8,128)(2,1)S(1)}, bf16[192,768]{1,0:T(8,128)(2,1)S(1)}, u32[]{:S(2)}, u32[]{:S(2)}) collective-permute-start(bf16[192,768]{1,0:T(8,128)(2,1)S(1)} %broadcast_select_fusion.2), channel_id=1, source_target_pairs={{0,248},{1,249},{2,250},{3,251},{4,252},{5,253},{6,254},{7,255},{8... | collective-permute-start | bytes 884744 | tf_op jit(solution)/shard_map/ppermute | solution.py:33
  101.3 1.5 collective-permute-start.15
  102.8 0.4 collective-permute-start.18
  103.3 4.4 %collective-permute-done.23.refs_17_ = bf16[192,768]{1,0:T(8,128)(2,1)S(1)} collective-permute-done((bf16[192,768]{1,0:T(8,128)(2,1)S(1)}, bf16[192,768]{1,0:T(8,128)(2,1)S(1)}, u32[]{:S(2)}, u32[]{:S(2)}) %collective-permute-start.23) | collective-permute-done | bytes 294944 | tf_op jit(solution)/shard_map/ppermute | solution.py:33
  107.7 1.4 collective-permute-start.22
  109.2 2.8 %collective-permute-start.21 = (bf16[192,768]{1,0:T(8,128)(2,1)S(1)}, bf16[192,768]{1,0:T(8,128)(2,1)S(1)}, u32[]{:S(2)}, u32[]{:S(2)}) collective-permute-start(bf16[192,768]{1,0:T(8,128)(2,1)S(1)} %collective-permute-done.20.refs_13_), channel_id=1, source_target_pairs={{0,8},{1,9},{2,10},{3,11},{4,12},{5,13},{6,14},{7,15},{8,0},{9,1},... | collective-permute-start | bytes 884744 | tf_op jit(solution)/shard_map/ppermute | solution.py:33
  111.9 0.1 collective-permute-start.24
  112.0 0.4 collective-permute-start.25
  112.5 0.7 collective-permute-done.21.refs_14_
  113.1 1.6 collective-permute-done.22.refs_15_
  114.7 3.6 %collective-permute-done.25.refs_19_ = bf16[192,768]{1,0:T(8,128)(2,1)S(1)} collective-permute-done((bf16[192,768]{1,0:T(8,128)(2,1)S(1)}, bf16[192,768]{1,0:T(8,128)(2,1)S(1)}, u32[]{:S(2)}, u32[]{:S(2)}) %collective-permute-start.25) | collective-permute-done | bytes 294944 | tf_op jit(solution)/shard_map/ppermute | solution.py:33
  118.4 13.8 %shard_map.41 = bf16[4,192,384]{2,1,0:T(8,128)(2,1)S(1)} custom-call(bf16[192,384]{1,0:T(8,128)(2,1)S(1)} %copy-done.2, bf16[192,384]{1,0:T(8,128)(2,1)S(1)} %get-tuple-element.14.refs_1_, bf16[192,384]{1,0:T(8,128)(2,1)S(1)} %get-tuple-element.15.refs_2_, bf16[192,384]{1,0:T(8,128)(2,1)S(1)} %get-tuple-element.16.refs_3_, ...), custom_call_target="tpu_custom_call" | custom-call | flops 3623878656 | bytes 4718592 | tf_op jit(solution)/shard_map/pallas_call | solution.py:157
  132.2 6.7 %collective-permute-start.31 = (bf16[192,384]{1,0:T(8,128)(2,1)S(1)}, bf16[192,384]{1,0:T(8,128)(2,1)S(1)}, u32[]{:S(2)}, u32[]{:S(2)}) collective-permute-start(bf16[192,384]{1,0:T(8,128)(2,1)S(1)} %get-tuple-element.26), channel_id=1, source_target_pairs={{0,4},{1,5},{2,6},{3,7},{4,0},{5,1},{6,2},{7,3},{8,12},{9,13},{10,... | collective-permute-start | bytes 442376 | tf_op jit(solution)/shard_map/ppermute | solution.py:33
  138.9 0.1 collective-permute-start.26
  139.0 3.3 %collective-permute-done.31 = bf16[192,384]{1,0:T(8,128)(2,1)S(1)} collective-permute-done((bf16[192,384]{1,0:T(8,128)(2,1)S(1)}, bf16[192,384]{1,0:T(8,128)(2,1)S(1)}, u32[]{:S(2)}, u32[]{:S(2)}) %collective-permute-start.31) | collective-permute-done | bytes 147488 | tf_op jit(solution)/shard_map/ppermute | solution.py:33
  142.3 2.4 %fusion.12 = f32[192,3072]{1,0:T(8,128)S(1)} fusion(bf16[192,384]{1,0:T(8,128)(2,1)S(1)} %collective-permute-done.31, bf16[384,3072]{1,0:T(8,128)(2,1)} %all-gather.2.cloned.1.call-done), kind=kOutput, calls=%fused_computation.28 | convolution fusion | flops 452984832 | bytes 4866048 | tf_op jit(solution)/shard_map/dot_general | solution.py:205
  144.8 0.8 fusion.10
  145.7 4.6 %collective-permute-start.33 = (bf16[48,3072]{1,0:T(8,128)(2,1)S(1)}, bf16[48,3072]{1,0:T(8,128)(2,1)S(1)}, u32[]{:S(2)}, u32[]{:S(2)}) collective-permute-start(bf16[48,3072]{1,0:T(8,128)(2,1)S(1)} %get-tuple-element.24), channel_id=1, source_target_pairs={{0,3},{1,0},{2,1},{3,2},{4,7},{5,4},{6,5},{7,6},{8,9},{9,10},{10,1... | collective-permute-start | bytes 884744 | tf_op jit(solution)/shard_map/ppermute | solution.py:33
  150.3 0.8 fusion.11
  151.1 0.8 fusion.9
  152.0 2.8 %collective-permute-start.29 = (bf16[48,3072]{1,0:T(8,128)(2,1)S(1)}, bf16[48,3072]{1,0:T(8,128)(2,1)S(1)}, u32[]{:S(2)}, u32[]{:S(2)}) collective-permute-start(bf16[48,3072]{1,0:T(8,128)(2,1)S(1)} %get-tuple-element.22), channel_id=1, source_target_pairs={{0,3},{1,0},{2,1},{3,2},{4,7},{5,4},{6,5},{7,6},{8,9},{9,10},{10,1... | collective-permute-start | bytes 884744 | tf_op jit(solution)/shard_map/ppermute | solution.py:33
  154.8 0.8 collective-permute-start.28
  155.6 0.1 fusion
  155.6 1.8 %collective-permute-start.34 = (bf16[48,3072]{1,0:T(8,128)(2,1)S(1)}, bf16[48,3072]{1,0:T(8,128)(2,1)S(1)}, u32[]{:S(2)}, u32[]{:S(2)}) collective-permute-start(bf16[48,3072]{1,0:T(8,128)(2,1)S(1)} %fusion), channel_id=1, source_target_pairs={{0,3},{1,0},{2,1},{3,2},{4,7},{5,4},{6,5},{7,6},{8,9},{9,10},{10,1... | collective-permute-start | bytes 884744 | tf_op jit(solution)/shard_map/ppermute | solution.py:33
  157.4 2.9 %collective-permute-done.29 = bf16[48,3072]{1,0:T(8,128)(2,1)S(1)} collective-permute-done((bf16[48,3072]{1,0:T(8,128)(2,1)S(1)}, bf16[48,3072]{1,0:T(8,128)(2,1)S(1)}, u32[]{:S(2)}, u32[]{:S(2)}) %collective-permute-start.29) | collective-permute-done | bytes 294944 | tf_op jit(solution)/shard_map/ppermute | solution.py:33
  160.3 0.1 fusion.3
  160.4 2.4 %collective-permute-start.30 = (bf16[48,3072]{1,0:T(8,128)(2,1)S(1)}, bf16[48,3072]{1,0:T(8,128)(2,1)S(1)}, u32[]{:S(2)}, u32[]{:S(2)}) collective-permute-start(bf16[48,3072]{1,0:T(8,128)(2,1)S(1)} %fusion.3), channel_id=1, source_target_pairs={{0,3},{1,0},{2,1},{3,2},{4,7},{5,4},{6,5},{7,6},{8,9},{9,10},{10,1... | collective-permute-start | bytes 884744 | tf_op jit(solution)/shard_map/ppermute | solution.py:33
  162.8 3.8 %collective-permute-done.34 = bf16[48,3072]{1,0:T(8,128)(2,1)S(1)} collective-permute-done((bf16[48,3072]{1,0:T(8,128)(2,1)S(1)}, bf16[48,3072]{1,0:T(8,128)(2,1)S(1)}, u32[]{:S(2)}, u32[]{:S(2)}) %collective-permute-start.34) | collective-permute-done | bytes 294944 | tf_op jit(solution)/shard_map/ppermute | solution.py:33
  166.6 0.1 fusion.2
  166.7 5.2 %collective-permute-done.30 = bf16[48,3072]{1,0:T(8,128)(2,1)S(1)} collective-permute-done((bf16[48,3072]{1,0:T(8,128)(2,1)S(1)}, bf16[48,3072]{1,0:T(8,128)(2,1)S(1)}, u32[]{:S(2)}, u32[]{:S(2)}) %collective-permute-start.30) | collective-permute-done | bytes 294944 | tf_op jit(solution)/shard_map/ppermute | solution.py:33
  171.9 0.1 fusion.5
  172.0 0.9 pad_maximum_fusion
  (42 shorter events, 0.3 us)
Async XLA Ops:
  6.5 1.7 copy-start
  6.5 135.8 %all-gather.2.cloned.1.call-start = ((), (), s32[]{:S(2)}) async-start(), calls=%async_computation | async-start | bytes 2654208 | tf_op jit(solution)/shard_map/all_gather | solution.py:199
  8.2 15.0 %collective-permute-start.27 = (bf16[48,3072]{1,0:T(8,128)(2,1)S(1)}, bf16[48,3072]{1,0:T(8,128)(2,1)S(1)}, u32[]{:S(2)}, u32[]{:S(2)}) collective-permute-start(bf16[48,3072]{1,0:T(8,128)(2,1)S(1)} %constant_dynamic-slice_fusion), channel_id=1, source_target_pairs={{0,4},{1,5},{2,6},{3,7},{4,0},{5,1},{6,2},{7,3},{8,12},{9,13},{10,... | collective-permute-start | bytes 884744 | tf_op jit(solution)/shard_map/ppermute | solution.py:33
  23.2 0.7 copy-start.4
  25.1 11.2 %collective-permute-start = (bf16[48,3072]{1,0:T(8,128)(2,1)S(1)}, bf16[48,3072]{1,0:T(8,128)(2,1)S(1)}, u32[]{:S(2)}, u32[]{:S(2)}) collective-permute-start(bf16[48,3072]{1,0:T(8,128)(2,1)S(1)} %get-tuple-element.28.own), channel_id=1, source_target_pairs={{0,1},{1,2},{2,3},{3,0},{4,5},{5,6},{6,7},{7,4},{8,11},{9,8},{10,9... | collective-permute-start | bytes 884744 | tf_op jit(solution)/shard_map/ppermute | solution.py:33
  28.2 10.3 %collective-permute-start.1 = (bf16[48,3072]{1,0:T(8,128)(2,1)S(1)}, bf16[48,3072]{1,0:T(8,128)(2,1)S(1)}, u32[]{:S(2)}, u32[]{:S(2)}) collective-permute-start(bf16[48,3072]{1,0:T(8,128)(2,1)S(1)} %get-tuple-element.28.own), channel_id=1, source_target_pairs={{0,3},{1,0},{2,1},{3,2},{4,7},{5,4},{6,5},{7,6},{8,9},{9,10},{10,1... | collective-permute-start | bytes 884744 | tf_op jit(solution)/shard_map/ppermute | solution.py:33
  28.2 10.3 %collective-permute-start.3 = (bf16[48,3072]{1,0:T(8,128)(2,1)S(1)}, bf16[48,3072]{1,0:T(8,128)(2,1)}, u32[]{:S(2)}, u32[]{:S(2)}) collective-permute-start(bf16[48,3072]{1,0:T(8,128)(2,1)S(1)} %get-tuple-element.27.own), channel_id=1, source_target_pairs={{0,1},{1,2},{2,3},{3,0},{4,5},{5,6},{6,7},{7,4},{8,11},{9,8},{10,9... | collective-permute-start | bytes 884744 | tf_op jit(solution)/shard_map/ppermute | solution.py:33
  30.8 10.5 %collective-permute-start.6 = (bf16[48,3072]{1,0:T(8,128)(2,1)S(1)}, bf16[48,3072]{1,0:T(8,128)(2,1)S(1)}, u32[]{:S(2)}, u32[]{:S(2)}) collective-permute-start(bf16[48,3072]{1,0:T(8,128)(2,1)S(1)} %get-tuple-element.28.own), channel_id=1, source_target_pairs={{0,4},{1,5},{2,6},{3,7},{4,0},{5,1},{6,2},{7,3},{8,12},{9,13},{10,... | collective-permute-start | bytes 884744 | tf_op jit(solution)/shard_map/ppermute | solution.py:33
  35.9 12.8 %collective-permute-start.10 = (bf16[48,3072]{1,0:T(8,128)(2,1)S(1)}, bf16[48,3072]{1,0:T(8,128)(2,1)S(1)}, u32[]{:S(2)}, u32[]{:S(2)}) collective-permute-start(bf16[48,3072]{1,0:T(8,128)(2,1)S(1)} %get-tuple-element.27.own), channel_id=1, source_target_pairs={{0,4},{1,5},{2,6},{3,7},{4,0},{5,1},{6,2},{7,3},{8,12},{9,13},{10,... | collective-permute-start | bytes 884744 | tf_op jit(solution)/shard_map/ppermute | solution.py:33
  36.2 12.5 %collective-permute-start.2 = (bf16[48,3072]{1,0:T(8,128)(2,1)S(1)}, bf16[48,3072]{1,0:T(8,128)(2,1)S(1)}, u32[]{:S(2)}, u32[]{:S(2)}) collective-permute-start(bf16[48,3072]{1,0:T(8,128)(2,1)S(1)} %collective-permute-done.first), channel_id=1, source_target_pairs={{0,1},{1,2},{2,3},{3,0},{4,5},{5,6},{6,7},{7,4},{8,11},{9,8},{10,9... | collective-permute-start | bytes 884744 | tf_op jit(solution)/shard_map/ppermute | solution.py:33
  38.4 25.0 %collective-permute-start.4 = (bf16[48,3072]{1,0:T(8,128)(2,1)S(1)}, bf16[48,3072]{1,0:T(8,128)(2,1)}, u32[]{:S(2)}, u32[]{:S(2)}) collective-permute-start(bf16[48,3072]{1,0:T(8,128)(2,1)S(1)} %get-tuple-element.27.own), channel_id=1, source_target_pairs={{0,3},{1,0},{2,1},{3,2},{4,7},{5,4},{6,5},{7,6},{8,9},{9,10},{10,1... | collective-permute-start | bytes 884744 | tf_op jit(solution)/shard_map/ppermute | solution.py:33
  38.5 25.3 %collective-permute-start.5 = (bf16[48,3072]{1,0:T(8,128)(2,1)}, bf16[48,3072]{1,0:T(8,128)(2,1)}, u32[]{:S(2)}, u32[]{:S(2)}) collective-permute-start(bf16[48,3072]{1,0:T(8,128)(2,1)} %collective-permute-done.3.first), channel_id=1, source_target_pairs={{0,1},{1,2},{2,3},{3,0},{4,5},{5,6},{6,7},{7,4},{8,11},{9,8},{10,9... | collective-permute-start | bytes 884744 | tf_op jit(solution)/shard_map/ppermute | solution.py:33
  41.4 22.9 %collective-permute-start.7 = (bf16[48,3072]{1,0:T(8,128)(2,1)S(1)}, bf16[48,3072]{1,0:T(8,128)(2,1)}, u32[]{:S(2)}, u32[]{:S(2)}) collective-permute-start(bf16[48,3072]{1,0:T(8,128)(2,1)S(1)} %collective-permute-done.6.own), channel_id=1, source_target_pairs={{0,1},{1,2},{2,3},{3,0},{4,5},{5,6},{6,7},{7,4},{8,11},{9,8},{10,9... | collective-permute-start | bytes 884744 | tf_op jit(solution)/shard_map/ppermute | solution.py:33
  48.7 23.0 %collective-permute-start.11 = (bf16[48,3072]{1,0:T(8,128)(2,1)S(1)}, bf16[48,3072]{1,0:T(8,128)(2,1)S(1)}, u32[]{:S(2)}, u32[]{:S(2)}) collective-permute-start(bf16[48,3072]{1,0:T(8,128)(2,1)S(1)} %collective-permute-done.10.own), channel_id=1, source_target_pairs={{0,1},{1,2},{2,3},{3,0},{4,5},{5,6},{6,7},{7,4},{8,11},{9,8},{10,9... | collective-permute-start | bytes 884744 | tf_op jit(solution)/shard_map/ppermute | solution.py:33
  54.5 0.7 copy-start.1
  55.2 17.1 %collective-permute-start.14 = (bf16[192,768]{1,0:T(8,128)(2,1)}, bf16[192,768]{1,0:T(8,128)(2,1)}, u32[]{:S(2)}, u32[]{:S(2)}) collective-permute-start(bf16[192,768]{1,0:T(8,128)(2,1)} %get-tuple-element.17.refs_4_), channel_id=1, source_target_pairs={{0,240},{1,241},{2,242},{3,243},{4,244},{5,245},{6,246},{7,247},{8... | collective-permute-start | bytes 884744 | tf_op jit(solution)/shard_map/ppermute | solution.py:33
  63.4 11.0 %collective-permute-start.8 = (bf16[48,3072]{1,0:T(8,128)(2,1)S(1)}, bf16[48,3072]{1,0:T(8,128)(2,1)S(1)}, u32[]{:S(2)}, u32[]{:S(2)}) collective-permute-start(bf16[48,3072]{1,0:T(8,128)(2,1)S(1)} %collective-permute-done.6.own), channel_id=1, source_target_pairs={{0,3},{1,0},{2,1},{3,2},{4,7},{5,4},{6,5},{7,6},{8,9},{9,10},{10,1... | collective-permute-start | bytes 884744 | tf_op jit(solution)/shard_map/ppermute | solution.py:33
  63.8 29.7 %collective-permute-start.12 = (bf16[48,3072]{1,0:T(8,128)(2,1)S(1)}, bf16[48,3072]{1,0:T(8,128)(2,1)S(1)}, u32[]{:S(2)}, u32[]{:S(2)}) collective-permute-start(bf16[48,3072]{1,0:T(8,128)(2,1)S(1)} %collective-permute-done.10.own), channel_id=1, source_target_pairs={{0,3},{1,0},{2,1},{3,2},{4,7},{5,4},{6,5},{7,6},{8,9},{9,10},{10,1... | collective-permute-start | bytes 884744 | tf_op jit(solution)/shard_map/ppermute | solution.py:33
  64.3 23.9 %collective-permute-start.9 = (bf16[48,3072]{1,0:T(8,128)(2,1)}, bf16[48,3072]{1,0:T(8,128)(2,1)S(1)}, u32[]{:S(2)}, u32[]{:S(2)}) collective-permute-start(bf16[48,3072]{1,0:T(8,128)(2,1)} %collective-permute-done.7.first), channel_id=1, source_target_pairs={{0,1},{1,2},{2,3},{3,0},{4,5},{5,6},{6,7},{7,4},{8,11},{9,8},{10,9... | collective-permute-start | bytes 884744 | tf_op jit(solution)/shard_map/ppermute | solution.py:33
  71.7 27.1 %collective-permute-start.17 = (bf16[192,768]{1,0:T(8,128)(2,1)S(1)}, bf16[192,768]{1,0:T(8,128)(2,1)S(1)}, u32[]{:S(2)}, u32[]{:S(2)}) collective-permute-start(bf16[192,768]{1,0:T(8,128)(2,1)S(1)} %get-tuple-element.18.refs_8_), channel_id=1, source_target_pairs={{0,240},{1,241},{2,242},{3,243},{4,244},{5,245},{6,246},{7,247},{8... | collective-permute-start | bytes 884744 | tf_op jit(solution)/shard_map/ppermute | solution.py:33
  72.3 21.3 %collective-permute-start.13 = (bf16[48,3072]{1,0:T(8,128)(2,1)S(1)}, bf16[48,3072]{1,0:T(8,128)(2,1)S(1)}, u32[]{:S(2)}, u32[]{:S(2)}) collective-permute-start(bf16[48,3072]{1,0:T(8,128)(2,1)S(1)} %collective-permute-done.11.first), channel_id=1, source_target_pairs={{0,1},{1,2},{2,3},{3,0},{4,5},{5,6},{6,7},{7,4},{8,11},{9,8},{10,9... | collective-permute-start | bytes 884744 | tf_op jit(solution)/shard_map/ppermute | solution.py:33
  74.4 37.6 %collective-permute-start.16 = (bf16[192,768]{1,0:T(8,128)(2,1)S(1)}, bf16[192,768]{1,0:T(8,128)(2,1)S(1)}, u32[]{:S(2)}, u32[]{:S(2)}) collective-permute-start(bf16[192,768]{1,0:T(8,128)(2,1)S(1)} %broadcast_select_fusion.3), channel_id=1, source_target_pairs={{0,248},{1,249},{2,250},{3,251},{4,252},{5,253},{6,254},{7,255},{8... | collective-permute-start | bytes 884744 | tf_op jit(solution)/shard_map/ppermute | solution.py:33
  93.3 9.5 %collective-permute-start.20 = (bf16[192,768]{1,0:T(8,128)(2,1)S(1)}, bf16[192,768]{1,0:T(8,128)(2,1)S(1)}, u32[]{:S(2)}, u32[]{:S(2)}) collective-permute-start(bf16[192,768]{1,0:T(8,128)(2,1)S(1)} %get-tuple-element.19.refs_12_), channel_id=1, source_target_pairs={{0,240},{1,241},{2,242},{3,243},{4,244},{5,245},{6,246},{7,247},{8... | collective-permute-start | bytes 884744 | tf_op jit(solution)/shard_map/ppermute | solution.py:33
  98.6 19.8 %copy-start.2 = (bf16[192,384]{1,0:T(8,128)(2,1)S(1)}, bf16[192,384]{1,0:T(8,128)(2,1)}, u32[]{:S(2)}) copy-start(bf16[192,384]{1,0:T(8,128)(2,1)} %copy-done.1) | copy-start | bytes 442372
  98.6 9.1 %collective-permute-start.23 = (bf16[192,768]{1,0:T(8,128)(2,1)S(1)}, bf16[192,768]{1,0:T(8,128)(2,1)S(1)}, u32[]{:S(2)}, u32[]{:S(2)}) collective-permute-start(bf16[192,768]{1,0:T(8,128)(2,1)S(1)} %get-tuple-element.20.refs_16_), channel_id=1, source_target_pairs={{0,240},{1,241},{2,242},{3,243},{4,244},{5,245},{6,246},{7,247},{8... | collective-permute-start | bytes 884744 | tf_op jit(solution)/shard_map/ppermute | solution.py:33
  98.9 13.5 %collective-permute-start.19 = (bf16[192,768]{1,0:T(8,128)(2,1)S(1)}, bf16[192,768]{1,0:T(8,128)(2,1)S(1)}, u32[]{:S(2)}, u32[]{:S(2)}) collective-permute-start(bf16[192,768]{1,0:T(8,128)(2,1)S(1)} %broadcast_select_fusion.2), channel_id=1, source_target_pairs={{0,248},{1,249},{2,250},{3,251},{4,252},{5,253},{6,254},{7,255},{8... | collective-permute-start | bytes 884744 | tf_op jit(solution)/shard_map/ppermute | solution.py:33
  101.3 7.9 %collective-permute-start.15 = (bf16[192,768]{1,0:T(8,128)(2,1)}, bf16[192,768]{1,0:T(8,128)(2,1)S(1)}, u32[]{:S(2)}, u32[]{:S(2)}) collective-permute-start(bf16[192,768]{1,0:T(8,128)(2,1)} %collective-permute-done.14.refs_5_), channel_id=1, source_target_pairs={{0,8},{1,9},{2,10},{3,11},{4,12},{5,13},{6,14},{7,15},{8,0},{9,1},... | collective-permute-start | bytes 884744 | tf_op jit(solution)/shard_map/ppermute | solution.py:33
  102.8 9.2 %collective-permute-start.18 = (bf16[192,768]{1,0:T(8,128)(2,1)S(1)}, bf16[192,768]{1,0:T(8,128)(2,1)S(1)}, u32[]{:S(2)}, u32[]{:S(2)}) collective-permute-start(bf16[192,768]{1,0:T(8,128)(2,1)S(1)} %collective-permute-done.17.refs_9_), channel_id=1, source_target_pairs={{0,8},{1,9},{2,10},{3,11},{4,12},{5,13},{6,14},{7,15},{8,0},{9,1},... | collective-permute-start | bytes 884744 | tf_op jit(solution)/shard_map/ppermute | solution.py:33
  107.7 7.1 %collective-permute-start.22 = (bf16[192,768]{1,0:T(8,128)(2,1)S(1)}, bf16[192,768]{1,0:T(8,128)(2,1)S(1)}, u32[]{:S(2)}, u32[]{:S(2)}) collective-permute-start(bf16[192,768]{1,0:T(8,128)(2,1)S(1)} %broadcast_select_fusion.1), channel_id=1, source_target_pairs={{0,248},{1,249},{2,250},{3,251},{4,252},{5,253},{6,254},{7,255},{8... | collective-permute-start | bytes 884744 | tf_op jit(solution)/shard_map/ppermute | solution.py:33
  109.2 4.0 %collective-permute-start.21 = (bf16[192,768]{1,0:T(8,128)(2,1)S(1)}, bf16[192,768]{1,0:T(8,128)(2,1)S(1)}, u32[]{:S(2)}, u32[]{:S(2)}) collective-permute-start(bf16[192,768]{1,0:T(8,128)(2,1)S(1)} %collective-permute-done.20.refs_13_), channel_id=1, source_target_pairs={{0,8},{1,9},{2,10},{3,11},{4,12},{5,13},{6,14},{7,15},{8,0},{9,1},... | collective-permute-start | bytes 884744 | tf_op jit(solution)/shard_map/ppermute | solution.py:33
  111.9 2.8 %collective-permute-start.24 = (bf16[192,768]{1,0:T(8,128)(2,1)S(1)}, bf16[192,768]{1,0:T(8,128)(2,1)S(1)}, u32[]{:S(2)}, u32[]{:S(2)}) collective-permute-start(bf16[192,768]{1,0:T(8,128)(2,1)S(1)} %collective-permute-done.23.refs_17_), channel_id=1, source_target_pairs={{0,8},{1,9},{2,10},{3,11},{4,12},{5,13},{6,14},{7,15},{8,0},{9,1},... | collective-permute-start | bytes 884744 | tf_op jit(solution)/shard_map/ppermute | solution.py:33
  112.0 6.3 %collective-permute-start.25 = (bf16[192,768]{1,0:T(8,128)(2,1)S(1)}, bf16[192,768]{1,0:T(8,128)(2,1)S(1)}, u32[]{:S(2)}, u32[]{:S(2)}) collective-permute-start(bf16[192,768]{1,0:T(8,128)(2,1)S(1)} %broadcast_select_fusion), channel_id=1, source_target_pairs={{0,248},{1,249},{2,250},{3,251},{4,252},{5,253},{6,254},{7,255},{8... | collective-permute-start | bytes 884744 | tf_op jit(solution)/shard_map/ppermute | solution.py:33
  132.2 10.1 %collective-permute-start.31 = (bf16[192,384]{1,0:T(8,128)(2,1)S(1)}, bf16[192,384]{1,0:T(8,128)(2,1)S(1)}, u32[]{:S(2)}, u32[]{:S(2)}) collective-permute-start(bf16[192,384]{1,0:T(8,128)(2,1)S(1)} %get-tuple-element.26), channel_id=1, source_target_pairs={{0,4},{1,5},{2,6},{3,7},{4,0},{5,1},{6,2},{7,3},{8,12},{9,13},{10,... | collective-permute-start | bytes 442376 | tf_op jit(solution)/shard_map/ppermute | solution.py:33
  138.9 11.4 %collective-permute-start.26 = (bf16[192,384]{1,0:T(8,128)(2,1)S(1)}, bf16[192,384]{1,0:T(8,128)(2,1)S(1)}, u32[]{:S(2)}, u32[]{:S(2)}) collective-permute-start(bf16[192,384]{1,0:T(8,128)(2,1)S(1)} %get-tuple-element.25), channel_id=1, source_target_pairs={{0,4},{1,5},{2,6},{3,7},{4,0},{5,1},{6,2},{7,3},{8,12},{9,13},{10,... | collective-permute-start | bytes 442376 | tf_op jit(solution)/shard_map/ppermute | solution.py:33
  144.8 5.5 %copy-start.3 = (bf16[384,3072]{1,0:T(8,128)(2,1)S(1)}, bf16[384,3072]{1,0:T(8,128)(2,1)}, u32[]{:S(2)}) copy-start(bf16[384,3072]{1,0:T(8,128)(2,1)} %all-gather.2.cloned.1.call-done) | copy-start | bytes 7077892
  145.7 9.9 %collective-permute-start.33 = (bf16[48,3072]{1,0:T(8,128)(2,1)S(1)}, bf16[48,3072]{1,0:T(8,128)(2,1)S(1)}, u32[]{:S(2)}, u32[]{:S(2)}) collective-permute-start(bf16[48,3072]{1,0:T(8,128)(2,1)S(1)} %get-tuple-element.24), channel_id=1, source_target_pairs={{0,3},{1,0},{2,1},{3,2},{4,7},{5,4},{6,5},{7,6},{8,9},{9,10},{10,1... | collective-permute-start | bytes 884744 | tf_op jit(solution)/shard_map/ppermute | solution.py:33
  150.3 12.5 %collective-permute-start.32 = (bf16[48,3072]{1,0:T(8,128)(2,1)S(1)}, bf16[48,3072]{1,0:T(8,128)(2,1)S(1)}, u32[]{:S(2)}, u32[]{:S(2)}) collective-permute-start(bf16[48,3072]{1,0:T(8,128)(2,1)S(1)} %get-tuple-element.23), channel_id=1, source_target_pairs={{0,1},{1,2},{2,3},{3,0},{4,5},{5,6},{6,7},{7,4},{8,11},{9,8},{10,9... | collective-permute-start | bytes 884744 | tf_op jit(solution)/shard_map/ppermute | solution.py:33
  152.0 8.3 %collective-permute-start.29 = (bf16[48,3072]{1,0:T(8,128)(2,1)S(1)}, bf16[48,3072]{1,0:T(8,128)(2,1)S(1)}, u32[]{:S(2)}, u32[]{:S(2)}) collective-permute-start(bf16[48,3072]{1,0:T(8,128)(2,1)S(1)} %get-tuple-element.22), channel_id=1, source_target_pairs={{0,3},{1,0},{2,1},{3,2},{4,7},{5,4},{6,5},{7,6},{8,9},{9,10},{10,1... | collective-permute-start | bytes 884744 | tf_op jit(solution)/shard_map/ppermute | solution.py:33
  154.8 12.0 %collective-permute-start.28 = (bf16[48,3072]{1,0:T(8,128)(2,1)S(1)}, bf16[48,3072]{1,0:T(8,128)(2,1)S(1)}, u32[]{:S(2)}, u32[]{:S(2)}) collective-permute-start(bf16[48,3072]{1,0:T(8,128)(2,1)S(1)} %get-tuple-element.21), channel_id=1, source_target_pairs={{0,1},{1,2},{2,3},{3,0},{4,5},{5,6},{6,7},{7,4},{8,11},{9,8},{10,9... | collective-permute-start | bytes 884744 | tf_op jit(solution)/shard_map/ppermute | solution.py:33
  155.6 11.0 %collective-permute-start.34 = (bf16[48,3072]{1,0:T(8,128)(2,1)S(1)}, bf16[48,3072]{1,0:T(8,128)(2,1)S(1)}, u32[]{:S(2)}, u32[]{:S(2)}) collective-permute-start(bf16[48,3072]{1,0:T(8,128)(2,1)S(1)} %fusion), channel_id=1, source_target_pairs={{0,3},{1,0},{2,1},{3,2},{4,7},{5,4},{6,5},{7,6},{8,9},{9,10},{10,1... | collective-permute-start | bytes 884744 | tf_op jit(solution)/shard_map/ppermute | solution.py:33
  160.4 11.5 %collective-permute-start.30 = (bf16[48,3072]{1,0:T(8,128)(2,1)S(1)}, bf16[48,3072]{1,0:T(8,128)(2,1)S(1)}, u32[]{:S(2)}, u32[]{:S(2)}) collective-permute-start(bf16[48,3072]{1,0:T(8,128)(2,1)S(1)} %fusion.3), channel_id=1, source_target_pairs={{0,3},{1,0},{2,1},{3,2},{4,7},{5,4},{6,5},{7,6},{8,9},{9,10},{10,1... | collective-permute-start | bytes 884744 | tf_op jit(solution)/shard_map/ppermute | solution.py:33
Sparse Core Ops, SparseCore 0:
  24.1 36.0 all-gather.1
